TPU v7x, 256 devices: a whole 4x4x8 slice. The times are simulated.
256 devices in a mesh: dp: 128 (over y, x, z), head: 2 (over core).
Axes of the slice: x: 4, y: 4, z: 8, core: 2. Of those that a mesh axis runs over, the one named last changes fastest.
Arguments:
- queries: bfloat16 [16384, 12288], P('dp', 'head'), may hold values from -128 to 128
- keys: bfloat16 [16384, 1024], P('dp', 'head'), may hold values from -6 to 6
- values: bfloat16 [16384, 1024], P('dp', 'head'), may hold values from -6 to 6
- grad_out: bfloat16 [16384, 12288], P(('dp', 'head')), may hold values from -6 to 6
- segments: int32 [16384], replicated, may hold values from 0 to 31, never falling along the last dimension, each value on 1 to 1024 neighbouring positions
Outputs:
- attention_out: bfloat16 [16384, 12288], P(('dp', 'head'))
- grad_queries: bfloat16 [16384, 12288], P('dp', 'head')
- grad_keys: bfloat16 [16384, 1024], P('dp', 'head')
- grad_values: bfloat16 [16384, 1024], P('dp', 'head')
Inputs may be any that keep to these rules, and one draw needn't show every extreme that they name: segments never fall; each document holds 1 to 1024 tokens and one holds exactly 1024.
All inputs are finite; a program needn't handle non-finite values.
Results may differ from a plain program's by a relative error of at most 0.011.
Values may be sent and summed in bfloat16 or wider, within the bound.
No kernel may reach another device: no remote copies, remote signals or barrier semaphores. Data moves between devices by JAX's collectives and lax.ppermute only.
A program may use at most 128 MiB of HBM per device.

v0:
```python
import math

import jax
import jax.numpy as jnp
from jax import lax
from jax.sharding import PartitionSpec as P

QHEADS = 96
KVHEADS = 8
HEAD_DIM = 128
DEPTH = 8


def from_behind(value, axis, steps):
    count = lax.axis_size(axis)
    first, last = (max(0, -steps), min(count, count - steps))
    return lax.ppermute(value, axis, [(source, source + steps) for source in range(first, last)])


def attend(query_heads, cotangent_heads, key_blocks, value_blocks, allowed_blocks):
    head_size = query_heads.shape[2]
    softmax_scale = 1.0 / math.sqrt(head_size)
    raw_scores = jnp.einsum(
        "rgd,jwd->jgrw", query_heads, key_blocks, preferred_element_type=jnp.float32
    )
    scores = jnp.where(allowed_blocks[:, None], softmax_scale * raw_scores, -jnp.inf)
    row_max = jnp.max(scores, axis=(0, 3), keepdims=True)
    exp_total = jnp.sum(jnp.exp(scores - row_max), axis=(0, 3), keepdims=True)
    log_total = row_max + jnp.log(exp_total)
    weights = jnp.exp(scores - log_total)
    weights_low = weights.astype(jnp.bfloat16)
    out_heads = jnp.einsum(
        "jgrw,jwd->rgd", weights_low, value_blocks, preferred_element_type=jnp.float32
    )
    out_low = lax.optimization_barrier(out_heads.astype(jnp.bfloat16))
    row_delta = jnp.sum(cotangent_heads.astype(jnp.float32) * out_low.astype(jnp.float32), axis=2)
    grad_weights = jnp.einsum(
        "rgd,jwd->jgrw", cotangent_heads, value_blocks, preferred_element_type=jnp.float32
    )
    grad_scores = (weights * (grad_weights - row_delta.T[None, :, :, None])).astype(jnp.bfloat16)
    query_term = jnp.einsum(
        "jgrw,jwd->rgd", grad_scores, key_blocks, preferred_element_type=jnp.float32
    )
    key_term = jnp.einsum(
        "jgrw,rgd->jwd", grad_scores, query_heads, preferred_element_type=jnp.float32
    )
    value_term = jnp.einsum(
        "jgrw,rgd->jwd", weights_low, cotangent_heads, preferred_element_type=jnp.float32
    )
    grad_query = (softmax_scale * query_term).astype(jnp.bfloat16)
    return (out_low, grad_query, softmax_scale * key_term, value_term)


def block_mask(doc_ids, seg_pad, block_index, row_start, query_count, row_count, block_span):
    window = block_span * row_count
    padding = (block_span - 1) * row_count
    base_row = block_index * row_count
    seg_query = lax.dynamic_slice_in_dim(doc_ids, base_row + row_start, query_count, 0)
    seg_keys = lax.dynamic_slice_in_dim(seg_pad, base_row, window, 0)
    query_pos = base_row + row_start + jnp.arange(query_count, dtype=jnp.int32)
    key_pos = base_row - padding + jnp.arange(window, dtype=jnp.int32)
    allowed = (seg_query[:, None] == seg_keys[None, :]) & (key_pos[None, :] <= query_pos[:, None])
    allowed_blocks = jnp.transpose(allowed.reshape(query_count, block_span, row_count), (1, 0, 2))
    live_blocks = jnp.any(allowed_blocks, axis=(1, 2))
    return (allowed_blocks, live_blocks)


def run_heads(query_rows, cotangent_rows, key_window, value_window, allowed_blocks):
    query_count = query_rows.shape[0]
    block_span = key_window.shape[0]
    key_rows = key_window.shape[1]
    kv_columns = key_window.shape[2]
    local_kv = kv_columns // HEAD_DIM
    group_size = QHEADS // KVHEADS

    def head_step(head_index, state):
        out_buffer, dq_buffer, key_terms, value_terms = state
        column = head_index * group_size * HEAD_DIM
        query_heads = lax.dynamic_slice_in_dim(
            query_rows, column, group_size * HEAD_DIM, 1
        ).reshape(query_count, group_size, HEAD_DIM)
        cotangent_heads = lax.dynamic_slice_in_dim(
            cotangent_rows, column, group_size * HEAD_DIM, 1
        ).reshape(query_count, group_size, HEAD_DIM)
        key_blocks = lax.dynamic_slice_in_dim(key_window, head_index * HEAD_DIM, HEAD_DIM, 2)
        value_blocks = lax.dynamic_slice_in_dim(value_window, head_index * HEAD_DIM, HEAD_DIM, 2)
        out_heads, grad_query, key_term, value_term = attend(
            query_heads, cotangent_heads, key_blocks, value_blocks, allowed_blocks
        )
        out_buffer = lax.dynamic_update_slice_in_dim(
            out_buffer, out_heads.reshape(query_count, group_size * HEAD_DIM), column, 1
        )
        dq_buffer = lax.dynamic_update_slice_in_dim(
            dq_buffer, grad_query.reshape(query_count, group_size * HEAD_DIM), column, 1
        )
        key_terms = lax.dynamic_update_slice_in_dim(key_terms, key_term, head_index * HEAD_DIM, 2)
        value_terms = lax.dynamic_update_slice_in_dim(
            value_terms, value_term, head_index * HEAD_DIM, 2
        )
        return (out_buffer, dq_buffer, key_terms, value_terms)

    start_state = (
        jnp.zeros(query_rows.shape, jnp.bfloat16),
        jnp.zeros(query_rows.shape, jnp.bfloat16),
        jnp.zeros((block_span, key_rows, kv_columns), jnp.float32),
        jnp.zeros((block_span, key_rows, kv_columns), jnp.float32),
    )
    return lax.fori_loop(0, local_kv, head_step, start_state)


def body(queries, keys, values, grad_out, segments):
    row_count = queries.shape[0]
    block_span = DEPTH + 1
    padding = DEPTH * row_count
    my_index = lax.axis_index("dp")
    seg_pad = jnp.concatenate([jnp.full((padding,), -1, jnp.int32), segments])
    grad_heads = lax.all_to_all(grad_out, "head", split_axis=1, concat_axis=0, tiled=True)
    key_parts = []
    value_parts = []
    for distance in range(DEPTH, 0, -1):
        moved_key, moved_value = from_behind((keys, values), "dp", distance)
        key_parts.append(moved_key)
        value_parts.append(moved_value)
    key_parts.append(keys)
    value_parts.append(values)
    key_window = jnp.stack(key_parts)
    value_window = jnp.stack(value_parts)
    allowed_blocks, live_blocks = block_mask(
        segments, seg_pad, my_index, 0, row_count, row_count, block_span
    )
    out_buffer, grad_queries, key_terms, value_terms = run_heads(
        queries, grad_heads, key_window, value_window, allowed_blocks
    )
    summed_key = key_terms[DEPTH]
    summed_value = value_terms[DEPTH]
    for distance in range(1, DEPTH + 1):
        moved_key, moved_value = from_behind(
            (key_terms[DEPTH - distance], value_terms[DEPTH - distance]), "dp", -distance
        )
        summed_key = summed_key + moved_key
        summed_value = summed_value + moved_value
    attention_out = lax.all_to_all(out_buffer, "head", split_axis=0, concat_axis=1, tiled=True)
    return (
        attention_out,
        grad_queries,
        summed_key.astype(jnp.bfloat16),
        summed_value.astype(jnp.bfloat16),
    )


def solution(mesh):
    placed = (P("dp", "head"), P("dp", "head"), P("dp", "head"), P(("dp", "head"), None), P())
    return jax.shard_map(
        body,
        mesh=mesh,
        in_specs=placed,
        out_specs=(P(("dp", "head"), None), P("dp", "head"), P("dp", "head"), P("dp", "head")),
        check_vma=False,
    )
```

profile of v0, /device:TPU:25, one launch (start us, length us, event | category | flops | bytes accessed | tf_op | source)
XLA Modules:
  0.0 408.0 jit_solution(10594263702309542699)
XLA Ops:
  10.1 5.7 %collective-permute-start.5 = (bf16[128,512]{0,1:T(8,128)(2,1)S(1)}, bf16[128,512]{0,1:T(8,128)(2,1)S(1)}, u32[]{:S(2)}, u32[]{:S(2)}) collective-permute-start(bf16[128,512]{0,1:T(8,128)(2,1)S(1)} %copy.79), channel_id=1, source_target_pairs={{0,6},{2,8},{4,10},{6,12},{8,14},{10,16},{12,18},{14,20},{16,22},{... | collective-permute-start | bytes 393224 | tf_op jit(solution)/shard_map/ppermute | solution.py:17
  24.7 6.8 %all-to-all-start = ((bf16[64,2,6144]{2,0,1:T(8,128)(2,1)}), bf16[64,2,6144]{2,0,1:T(8,128)(2,1)}, u32[]{:S(2)}, u32[]{:S(2)}) async-start(bf16[64,2,6144]{2,0,1:T(8,128)(2,1)} %bitcast.207), calls=%async_computation | async-start | bytes 3145728 | tf_op jit(solution)/shard_map/all_to_all | solution.py:117
  40.5 6.4 %collective-permute-start.10 = (bf16[128,512]{1,0:T(8,128)(2,1)S(1)}, bf16[128,512]{1,0:T(8,128)(2,1)S(1)}, u32[]{:S(2)}, u32[]{:S(2)}) collective-permute-start(bf16[128,512]{1,0:T(8,128)(2,1)S(1)} %copy-done.7), channel_id=1, source_target_pairs={{0,12},{2,14},{4,16},{6,18},{8,20},{10,22},{12,24},{14,26},{16,28}... | collective-permute-start | bytes 393224 | tf_op jit(solution)/shard_map/ppermute | solution.py:17
  50.5 7.9 %collective-permute-start.11 = (bf16[128,512]{1,0:T(8,128)(2,1)S(1)}, bf16[128,512]{1,0:T(8,128)(2,1)S(1)}, u32[]{:S(2)}, u32[]{:S(2)}) collective-permute-start(bf16[128,512]{1,0:T(8,128)(2,1)S(1)} %copy-done.7), channel_id=1, source_target_pairs={{0,10},{2,12},{4,14},{6,16},{8,18},{10,20},{12,22},{14,24},{16,26}... | collective-permute-start | bytes 393224 | tf_op jit(solution)/shard_map/ppermute | solution.py:17
  59.0 7.4 %collective-permute-done.11 = bf16[128,512]{1,0:T(8,128)(2,1)S(1)} collective-permute-done((bf16[128,512]{1,0:T(8,128)(2,1)S(1)}, bf16[128,512]{1,0:T(8,128)(2,1)S(1)}, u32[]{:S(2)}, u32[]{:S(2)}) %collective-permute-start.11) | collective-permute-done | bytes 131104 | tf_op jit(solution)/shard_map/ppermute | solution.py:17
  66.5 10.5 %collective-permute-start.12 = (bf16[128,512]{1,0:T(8,128)(2,1)S(1)}, bf16[128,512]{1,0:T(8,128)(2,1)S(1)}, u32[]{:S(2)}, u32[]{:S(2)}) collective-permute-start(bf16[128,512]{1,0:T(8,128)(2,1)S(1)} %copy-done.7), channel_id=1, source_target_pairs={{0,8},{2,10},{4,12},{6,14},{8,16},{10,18},{12,20},{14,22},{16,24},... | collective-permute-start | bytes 393224 | tf_op jit(solution)/shard_map/ppermute | solution.py:17
  79.2 12.6 %collective-permute-start.13 = (bf16[128,512]{1,0:T(8,128)(2,1)S(1)}, bf16[128,512]{1,0:T(8,128)(2,1)S(1)}, u32[]{:S(2)}, u32[]{:S(2)}) collective-permute-start(bf16[128,512]{1,0:T(8,128)(2,1)S(1)} %copy-done.7), channel_id=1, source_target_pairs={{0,6},{2,8},{4,10},{6,12},{8,14},{10,16},{12,18},{14,20},{16,22},{... | collective-permute-start | bytes 393224 | tf_op jit(solution)/shard_map/ppermute | solution.py:17
  92.4 6.5 %collective-permute-done.13 = bf16[128,512]{1,0:T(8,128)(2,1)S(1)} collective-permute-done((bf16[128,512]{1,0:T(8,128)(2,1)S(1)}, bf16[128,512]{1,0:T(8,128)(2,1)S(1)}, u32[]{:S(2)}, u32[]{:S(2)}) %collective-permute-start.13) | collective-permute-done | bytes 131104 | tf_op jit(solution)/shard_map/ppermute | solution.py:17
  101.5 8.6 %collective-permute-done.14 = bf16[128,512]{1,0:T(8,128)(2,1)S(1)} collective-permute-done((bf16[128,512]{1,0:T(8,128)(2,1)S(1)}, bf16[128,512]{1,0:T(8,128)(2,1)S(1)}, u32[]{:S(2)}, u32[]{:S(2)}) %collective-permute-start.14) | collective-permute-done | bytes 131104 | tf_op jit(solution)/shard_map/ppermute | solution.py:17
  112.7 7.3 %collective-permute-done.15 = bf16[128,512]{1,0:T(8,128)(2,1)S(1)} collective-permute-done((bf16[128,512]{1,0:T(8,128)(2,1)S(1)}, bf16[128,512]{1,0:T(8,128)(2,1)S(1)}, u32[]{:S(2)}, u32[]{:S(2)}) %collective-permute-start.15) | collective-permute-done | bytes 131104 | tf_op jit(solution)/shard_map/ppermute | solution.py:17
  130.4 6.1 %collective-permute-done.1 = bf16[128,512]{0,1:T(8,128)(2,1)S(1)} collective-permute-done((bf16[128,512]{0,1:T(8,128)(2,1)S(1)}, bf16[128,512]{0,1:T(8,128)(2,1)S(1)}, u32[]{:S(2)}, u32[]{:S(2)}) %collective-permute-start.1) | collective-permute-done | bytes 131104 | tf_op jit(solution)/shard_map/ppermute | solution.py:17
  139.1 7.1 %collective-permute-done.2 = bf16[128,512]{0,1:T(8,128)(2,1)S(1)} collective-permute-done((bf16[128,512]{0,1:T(8,128)(2,1)S(1)}, bf16[128,512]{0,1:T(8,128)(2,1)S(1)}, u32[]{:S(2)}, u32[]{:S(2)}) %collective-permute-start.2) | collective-permute-done | bytes 131104 | tf_op jit(solution)/shard_map/ppermute | solution.py:17
  148.8 8.0 %collective-permute-done.3 = bf16[128,512]{0,1:T(8,128)(2,1)S(1)} collective-permute-done((bf16[128,512]{0,1:T(8,128)(2,1)S(1)}, bf16[128,512]{0,1:T(8,128)(2,1)S(1)}, u32[]{:S(2)}, u32[]{:S(2)}) %collective-permute-start.3) | collective-permute-done | bytes 131104 | tf_op jit(solution)/shard_map/ppermute | solution.py:17
  166.9 112.0 %while.22 = (s32[]{:T(128)}, bf16[128,6144]{1,0:T(8,128)(2,1)}, bf16[128,6144]{1,0:T(8,128)(2,1)}, f32[9,128,512]{2,1,0:T(8,128)}, f32[9,128,512]{2,1,0:T(8,128)...) while((s32[]{:T(128)}, bf16[128,6144]{1,0:T(8,128)(2,1)}, ...), condition=%wide.region_4.5_spmd.clone, body=%wide.region_0.4_spmd.clone.sunk | while | flops 2757030912 | bytes 114602480 | solution.py:108
  181.3 5.6 %fusion.88 = f32[9,128,512]{2,1,0:T(8,128)} fusion(f32[9,128,512]{2,1,0:T(8,128)} %get-tuple-element.496, s32[]{:T(128)S(6)} %select_n.72, bf16[128,12,128,1]{0,2,1,3:T(8,128)(2,1)} %bitcast.267, f32[9,128,128,12]{2,1,3,0:T(8,128)} %copy-done, f32[12,128]{1,0:T(8,128)S(1)} %log_add_fusion.2, pred[9,128,128]{1,2,0:T(8,128)(4,1)S(1)} %compare_and_fusion.2), kind=kOutput, calls=%fused_computation.13.clone.1 | convolution fusion | flops 460062720 | bytes 8214532 | tf_op jit(solution)/shard_map/while/body/eval_jaxpr/jgrw,rgd->jwd/dot_general | solution.py:47
  209.3 5.6 %fusion.88 = f32[9,128,512]{2,1,0:T(8,128)} fusion(f32[9,128,512]{2,1,0:T(8,128)} %get-tuple-element.496, s32[]{:T(128)S(6)} %select_n.72, bf16[128,12,128,1]{0,2,1,3:T(8,128)(2,1)} %bitcast.267, f32[9,128,128,12]{2,1,3,0:T(8,128)} %copy-done, f32[12,128]{1,0:T(8,128)S(1)} %log_add_fusion.2, pred[9,128,128]{1,2,0:T(8,128)(4,1)S(1)} %compare_and_fusion.2), kind=kOutput, calls=%fused_computation.13.clone.1 | convolution fusion | flops 460062720 | bytes 8214532 | tf_op jit(solution)/shard_map/while/body/eval_jaxpr/jgrw,rgd->jwd/dot_general | solution.py:47
  265.3 5.6 %fusion.88 = f32[9,128,512]{2,1,0:T(8,128)} fusion(f32[9,128,512]{2,1,0:T(8,128)} %get-tuple-element.496, s32[]{:T(128)S(6)} %select_n.72, bf16[128,12,128,1]{0,2,1,3:T(8,128)(2,1)} %bitcast.267, f32[9,128,128,12]{2,1,3,0:T(8,128)} %copy-done, f32[12,128]{1,0:T(8,128)S(1)} %log_add_fusion.2, pred[9,128,128]{1,2,0:T(8,128)(4,1)S(1)} %compare_and_fusion.2), kind=kOutput, calls=%fused_computation.13.clone.1 | convolution fusion | flops 460062720 | bytes 8214532 | tf_op jit(solution)/shard_map/while/body/eval_jaxpr/jgrw,rgd->jwd/dot_general | solution.py:47
  293.1 12.8 %collective-permute-start.26 = (f32[128,512]{1,0:T(8,128)S(1)}, f32[128,512]{1,0:T(8,128)S(1)}, u32[]{:S(2)}, u32[]{:S(2)}) collective-permute-start(f32[128,512]{1,0:T(8,128)S(1)} %get-tuple-element.375), channel_id=1, source_target_pairs={{6,0},{8,2},{10,4},{12,6},{14,8},{16,10},{18,12},{20,14},{22,16},{... | collective-permute-start | bytes 786440 | tf_op jit(solution)/shard_map/ppermute | solution.py:17
  319.5 6.2 %collective-permute-start.21 = (f32[128,512]{1,0:T(8,128)S(1)}, f32[128,512]{1,0:T(8,128)S(1)}, u32[]{:S(2)}, u32[]{:S(2)}) collective-permute-start(f32[128,512]{1,0:T(8,128)S(1)} %get-tuple-element.380), channel_id=1, source_target_pairs={{12,0},{14,2},{16,4},{18,6},{20,8},{22,10},{24,12},{26,14},{28,16}... | collective-permute-start | bytes 786440 | tf_op jit(solution)/shard_map/ppermute | solution.py:17
  325.8 27.0 %all_to_all.38 = bf16[2,64,6144]{2,1,0:T(8,128)(2,1)S(1)} all-to-all(bf16[2,64,6144]{2,1,0:T(8,128)(2,1)S(1)} %bitcast.271), channel_id=1, replica_groups=mesh['dp'=128,'head'=2] {'head'}, dimensions={0} | all-to-all | bytes 3145728 | tf_op jit(solution)/shard_map/all_to_all | solution.py:142
  354.0 7.7 %collective-permute-start.20 = (f32[128,512]{1,0:T(8,128)S(1)}, f32[128,512]{1,0:T(8,128)S(1)}, u32[]{:S(2)}, u32[]{:S(2)}) collective-permute-start(f32[128,512]{1,0:T(8,128)S(1)} %get-tuple-element.381), channel_id=1, source_target_pairs={{10,0},{12,2},{14,4},{16,6},{18,8},{20,10},{22,12},{24,14},{26,16}... | collective-permute-start | bytes 786440 | tf_op jit(solution)/shard_map/ppermute | solution.py:17
  378.3 6.1 %collective-permute-done.20 = f32[128,512]{1,0:T(8,128)S(1)} collective-permute-done((f32[128,512]{1,0:T(8,128)S(1)}, f32[128,512]{1,0:T(8,128)S(1)}, u32[]{:S(2)}, u32[]{:S(2)}) %collective-permute-start.20) | collective-permute-done | bytes 262176 | tf_op jit(solution)/shard_map/ppermute | solution.py:17
  384.3 5.6 %collective-permute-done.18 = f32[128,512]{1,0:T(8,128)S(1)} collective-permute-done((f32[128,512]{1,0:T(8,128)S(1)}, f32[128,512]{1,0:T(8,128)S(1)}, u32[]{:S(2)}, u32[]{:S(2)}) %collective-permute-start.18) | collective-permute-done | bytes 262176 | tf_op jit(solution)/shard_map/ppermute | solution.py:17
  389.9 17.2 %collective-permute-done.17 = f32[128,512]{1,0:T(8,128)S(1)} collective-permute-done((f32[128,512]{1,0:T(8,128)S(1)}, f32[128,512]{1,0:T(8,128)S(1)}, u32[]{:S(2)}, u32[]{:S(2)}) %collective-permute-start.17) | collective-permute-done | bytes 262176 | tf_op jit(solution)/shard_map/ppermute | solution.py:17
  (213 shorter events, 206.0 us)
Async XLA Ops:
  1.7 157.9 %collective-permute-start.7 = (bf16[128,512]{0,1:T(8,128)(2,1)S(1)}, bf16[128,512]{0,1:T(8,128)(2,1)S(1)}, u32[]{:S(2)}, u32[]{:S(2)}) collective-permute-start(bf16[128,512]{0,1:T(8,128)(2,1)S(1)} %copy.79), channel_id=1, source_target_pairs={{0,2},{2,4},{4,6},{6,8},{8,10},{10,12},{12,14},{14,16},{16,18},{18... | collective-permute-start | bytes 393224 | tf_op jit(solution)/shard_map/ppermute | solution.py:17
  5.2 153.6 %collective-permute-start.6 = (bf16[128,512]{0,1:T(8,128)(2,1)S(1)}, bf16[128,512]{0,1:T(8,128)(2,1)S(1)}, u32[]{:S(2)}, u32[]{:S(2)}) collective-permute-start(bf16[128,512]{0,1:T(8,128)(2,1)S(1)} %copy.79), channel_id=1, source_target_pairs={{0,4},{2,6},{4,8},{6,10},{8,12},{10,14},{12,16},{14,18},{16,20},{1... | collective-permute-start | bytes 393224 | tf_op jit(solution)/shard_map/ppermute | solution.py:17
  10.1 148.1 %collective-permute-start.5 = (bf16[128,512]{0,1:T(8,128)(2,1)S(1)}, bf16[128,512]{0,1:T(8,128)(2,1)S(1)}, u32[]{:S(2)}, u32[]{:S(2)}) collective-permute-start(bf16[128,512]{0,1:T(8,128)(2,1)S(1)} %copy.79), channel_id=1, source_target_pairs={{0,6},{2,8},{4,10},{6,12},{8,14},{10,16},{12,18},{14,20},{16,22},{... | collective-permute-start | bytes 393224 | tf_op jit(solution)/shard_map/ppermute | solution.py:17
  15.8 141.7 %collective-permute-start.4 = (bf16[128,512]{0,1:T(8,128)(2,1)S(1)}, bf16[128,512]{0,1:T(8,128)(2,1)S(1)}, u32[]{:S(2)}, u32[]{:S(2)}) collective-permute-start(bf16[128,512]{0,1:T(8,128)(2,1)S(1)} %copy.79), channel_id=1, source_target_pairs={{0,8},{2,10},{4,12},{6,14},{8,16},{10,18},{12,20},{14,22},{16,24},... | collective-permute-start | bytes 393224 | tf_op jit(solution)/shard_map/ppermute | solution.py:17
  18.9 12.8 %collective-permute-start.8 = (bf16[128,512]{1,0:T(8,128)(2,1)}, bf16[128,512]{1,0:T(8,128)(2,1)S(1)}, u32[]{:S(2)}, u32[]{:S(2)}) collective-permute-start(bf16[128,512]{1,0:T(8,128)(2,1)} %param.8), channel_id=1, source_target_pairs={{0,16},{2,18},{4,20},{6,22},{8,24},{10,26},{12,28},{14,30},{16,32}... | collective-permute-start | bytes 393224 | tf_op jit(solution)/shard_map/ppermute | solution.py:17
  24.7 136.1 %all-to-all-start = ((bf16[64,2,6144]{2,0,1:T(8,128)(2,1)}), bf16[64,2,6144]{2,0,1:T(8,128)(2,1)}, u32[]{:S(2)}, u32[]{:S(2)}) async-start(bf16[64,2,6144]{2,0,1:T(8,128)(2,1)} %bitcast.207), calls=%async_computation | async-start | bytes 3145728 | tf_op jit(solution)/shard_map/all_to_all | solution.py:117
  50.5 16.0 %collective-permute-start.11 = (bf16[128,512]{1,0:T(8,128)(2,1)S(1)}, bf16[128,512]{1,0:T(8,128)(2,1)S(1)}, u32[]{:S(2)}, u32[]{:S(2)}) collective-permute-start(bf16[128,512]{1,0:T(8,128)(2,1)S(1)} %copy-done.7), channel_id=1, source_target_pairs={{0,10},{2,12},{4,14},{6,16},{8,18},{10,20},{12,22},{14,24},{16,26}... | collective-permute-start | bytes 393224 | tf_op jit(solution)/shard_map/ppermute | solution.py:17
  66.5 12.7 %collective-permute-start.12 = (bf16[128,512]{1,0:T(8,128)(2,1)S(1)}, bf16[128,512]{1,0:T(8,128)(2,1)S(1)}, u32[]{:S(2)}, u32[]{:S(2)}) collective-permute-start(bf16[128,512]{1,0:T(8,128)(2,1)S(1)} %copy-done.7), channel_id=1, source_target_pairs={{0,8},{2,10},{4,12},{6,14},{8,16},{10,18},{12,20},{14,22},{16,24},... | collective-permute-start | bytes 393224 | tf_op jit(solution)/shard_map/ppermute | solution.py:17
  79.2 19.7 %collective-permute-start.13 = (bf16[128,512]{1,0:T(8,128)(2,1)S(1)}, bf16[128,512]{1,0:T(8,128)(2,1)S(1)}, u32[]{:S(2)}, u32[]{:S(2)}) collective-permute-start(bf16[128,512]{1,0:T(8,128)(2,1)S(1)} %copy-done.7), channel_id=1, source_target_pairs={{0,6},{2,8},{4,10},{6,12},{8,14},{10,16},{12,18},{14,20},{16,22},{... | collective-permute-start | bytes 393224 | tf_op jit(solution)/shard_map/ppermute | solution.py:17
  282.7 23.5 %collective-permute-start.30 = (f32[128,512]{1,0:T(8,128)S(1)}, f32[128,512]{1,0:T(8,128)S(1)}, u32[]{:S(2)}, u32[]{:S(2)}) collective-permute-start(f32[128,512]{1,0:T(8,128)S(1)} %get-tuple-element.371), channel_id=1, source_target_pairs={{14,0},{16,2},{18,4},{20,6},{22,8},{24,10},{26,12},{28,14},{30,16}... | collective-permute-start | bytes 786440 | tf_op jit(solution)/shard_map/ppermute | solution.py:17
  284.6 23.6 %collective-permute-start.29 = (f32[128,512]{1,0:T(8,128)S(1)}, f32[128,512]{1,0:T(8,128)S(1)}, u32[]{:S(2)}, u32[]{:S(2)}) collective-permute-start(f32[128,512]{1,0:T(8,128)S(1)} %get-tuple-element.372), channel_id=1, source_target_pairs={{12,0},{14,2},{16,4},{18,6},{20,8},{22,10},{24,12},{26,14},{28,16}... | collective-permute-start | bytes 786440 | tf_op jit(solution)/shard_map/ppermute | solution.py:17
  286.5 24.2 %collective-permute-start.28 = (f32[128,512]{1,0:T(8,128)S(1)}, f32[128,512]{1,0:T(8,128)S(1)}, u32[]{:S(2)}, u32[]{:S(2)}) collective-permute-start(f32[128,512]{1,0:T(8,128)S(1)} %get-tuple-element.373), channel_id=1, source_target_pairs={{10,0},{12,2},{14,4},{16,6},{18,8},{20,10},{22,12},{24,14},{26,16}... | collective-permute-start | bytes 786440 | tf_op jit(solution)/shard_map/ppermute | solution.py:17
  291.2 22.7 %collective-permute-start.27 = (f32[128,512]{1,0:T(8,128)S(1)}, f32[128,512]{1,0:T(8,128)S(1)}, u32[]{:S(2)}, u32[]{:S(2)}) collective-permute-start(f32[128,512]{1,0:T(8,128)S(1)} %get-tuple-element.374), channel_id=1, source_target_pairs={{8,0},{10,2},{12,4},{14,6},{16,8},{18,10},{20,12},{22,14},{24,16},... | collective-permute-start | bytes 786440 | tf_op jit(solution)/shard_map/ppermute | solution.py:17
  293.1 26.4 %collective-permute-start.26 = (f32[128,512]{1,0:T(8,128)S(1)}, f32[128,512]{1,0:T(8,128)S(1)}, u32[]{:S(2)}, u32[]{:S(2)}) collective-permute-start(f32[128,512]{1,0:T(8,128)S(1)} %get-tuple-element.375), channel_id=1, source_target_pairs={{6,0},{8,2},{10,4},{12,6},{14,8},{16,10},{18,12},{20,14},{22,16},{... | collective-permute-start | bytes 786440 | tf_op jit(solution)/shard_map/ppermute | solution.py:17
  306.2 47.9 %collective-permute-start.25 = (f32[128,512]{1,0:T(8,128)S(1)}, f32[128,512]{1,0:T(8,128)S(1)}, u32[]{:S(2)}, u32[]{:S(2)}) collective-permute-start(f32[128,512]{1,0:T(8,128)S(1)} %get-tuple-element.376), channel_id=1, source_target_pairs={{4,0},{6,2},{8,4},{10,6},{12,8},{14,10},{16,12},{18,14},{20,16},{2... | collective-permute-start | bytes 786440 | tf_op jit(solution)/shard_map/ppermute | solution.py:17
  308.3 53.5 %collective-permute-start.31 = (f32[128,512]{1,0:T(8,128)S(1)}, f32[128,512]{1,0:T(8,128)S(1)}, u32[]{:S(2)}, u32[]{:S(2)}) collective-permute-start(f32[128,512]{1,0:T(8,128)S(1)} %get-tuple-element.377), channel_id=1, source_target_pairs={{16,0},{18,2},{20,4},{22,6},{24,8},{26,10},{28,12},{30,14},{32,16}... | collective-permute-start | bytes 786440 | tf_op jit(solution)/shard_map/ppermute | solution.py:17
  310.8 56.3 %collective-permute-start.16 = (f32[128,512]{1,0:T(8,128)S(1)}, f32[128,512]{1,0:T(8,128)S(1)}, u32[]{:S(2)}, u32[]{:S(2)}) collective-permute-start(f32[128,512]{1,0:T(8,128)S(1)} %get-tuple-element.378), channel_id=1, source_target_pairs={{2,0},{4,2},{6,4},{8,6},{10,8},{12,10},{14,12},{16,14},{18,16},{20... | collective-permute-start | bytes 786440 | tf_op jit(solution)/shard_map/ppermute | solution.py:17
  313.9 57.8 %collective-permute-start.22 = (f32[128,512]{1,0:T(8,128)S(1)}, f32[128,512]{1,0:T(8,128)S(1)}, u32[]{:S(2)}, u32[]{:S(2)}) collective-permute-start(f32[128,512]{1,0:T(8,128)S(1)} %get-tuple-element.379), channel_id=1, source_target_pairs={{14,0},{16,2},{18,4},{20,6},{22,8},{24,10},{26,12},{28,14},{30,16}... | collective-permute-start | bytes 786440 | tf_op jit(solution)/shard_map/ppermute | solution.py:17
  319.5 54.1 %collective-permute-start.21 = (f32[128,512]{1,0:T(8,128)S(1)}, f32[128,512]{1,0:T(8,128)S(1)}, u32[]{:S(2)}, u32[]{:S(2)}) collective-permute-start(f32[128,512]{1,0:T(8,128)S(1)} %get-tuple-element.380), channel_id=1, source_target_pairs={{12,0},{14,2},{16,4},{18,6},{20,8},{22,10},{24,12},{26,14},{28,16}... | collective-permute-start | bytes 786440 | tf_op jit(solution)/shard_map/ppermute | solution.py:17
  354.0 30.3 %collective-permute-start.20 = (f32[128,512]{1,0:T(8,128)S(1)}, f32[128,512]{1,0:T(8,128)S(1)}, u32[]{:S(2)}, u32[]{:S(2)}) collective-permute-start(f32[128,512]{1,0:T(8,128)S(1)} %get-tuple-element.381), channel_id=1, source_target_pairs={{10,0},{12,2},{14,4},{16,6},{18,8},{20,10},{22,12},{24,14},{26,16}... | collective-permute-start | bytes 786440 | tf_op jit(solution)/shard_map/ppermute | solution.py:17
  361.7 22.6 %collective-permute-start.19 = (f32[128,512]{1,0:T(8,128)S(1)}, f32[128,512]{1,0:T(8,128)S(1)}, u32[]{:S(2)}, u32[]{:S(2)}) collective-permute-start(f32[128,512]{1,0:T(8,128)S(1)} %get-tuple-element.382), channel_id=1, source_target_pairs={{8,0},{10,2},{12,4},{14,6},{16,8},{18,10},{20,12},{22,14},{24,16},... | collective-permute-start | bytes 786440 | tf_op jit(solution)/shard_map/ppermute | solution.py:17
  367.1 22.8 %collective-permute-start.18 = (f32[128,512]{1,0:T(8,128)S(1)}, f32[128,512]{1,0:T(8,128)S(1)}, u32[]{:S(2)}, u32[]{:S(2)}) collective-permute-start(f32[128,512]{1,0:T(8,128)S(1)} %get-tuple-element.383), channel_id=1, source_target_pairs={{6,0},{8,2},{10,4},{12,6},{14,8},{16,10},{18,12},{20,14},{22,16},{... | collective-permute-start | bytes 786440 | tf_op jit(solution)/shard_map/ppermute | solution.py:17
  371.7 35.4 %collective-permute-start.17 = (f32[128,512]{1,0:T(8,128)S(1)}, f32[128,512]{1,0:T(8,128)S(1)}, u32[]{:S(2)}, u32[]{:S(2)}) collective-permute-start(f32[128,512]{1,0:T(8,128)S(1)} %get-tuple-element.384), channel_id=1, source_target_pairs={{4,0},{6,2},{8,4},{10,6},{12,8},{14,10},{16,12},{18,14},{20,16},{2... | collective-permute-start | bytes 786440 | tf_op jit(solution)/shard_map/ppermute | solution.py:17
  373.7 33.5 %collective-permute-start.23 = (f32[128,512]{1,0:T(8,128)S(1)}, f32[128,512]{1,0:T(8,128)S(1)}, u32[]{:S(2)}, u32[]{:S(2)}) collective-permute-start(f32[128,512]{1,0:T(8,128)S(1)} %get-tuple-element.385), channel_id=1, source_target_pairs={{16,0},{18,2},{20,4},{22,6},{24,8},{26,10},{28,12},{30,14},{32,16}... | collective-permute-start | bytes 786440 | tf_op jit(solution)/shard_map/ppermute | solution.py:17
  (41 other events, 263.2 us)
where the time goes:
time: 410 us; the launch traced here: 408 us
  starting transfers between devices  143 us (35%)
  waiting for transfers between devices  96.7 us (24%)
  matrix products  69.2 us (17%)
  local copies, waits for them, and re-layouts  59.2 us (14%)
  blocking collectives  27 us (7%)
  other arithmetic  10.8 us (3%)
    ppermute x32, starting transfers between devices, from_behind(): lax.ppermute(value, axis, [(source, source + steps) for source in range(f...  137 us
    ppermute x32, waiting for transfers between devices, from_behind(): lax.ppermute(value, axis, [(source, source + steps) for source in range(f...  96.7 us
    all_to_all x1, blocking collectives, body(): lax.all_to_all(out_buffer, 'head', split_axis=0, concat_axis=1, tiled=True)  27 us
    dot_general x4, matrix products, attend(): jnp.einsum('jgrw,rgd->jwd', weights_low, cotangent_heads, preferred_eleme...  22.3 us
    dot_general x4, matrix products, attend(): jnp.einsum('rgd,jwd->jgrw', cotangent_heads, value_blocks, preferred_elem...  12.6 us
    unnamed x25, local copies, waits for them, and re-layouts  11.6 us
    dot_general x4, matrix products, attend(): jnp.einsum('jgrw,jwd->rgd', weights_low, value_blocks, preferred_element_...  11.5 us
    dynamic_update_slice x4, local copies, waits for them, and re-layouts, head_step(): lax.dynamic_update_slice_in_dim(out_buffer, out_heads.reshape(query_count...  8.83 us
  transfers between devices with their start and end apart: 33, of which 15 were waited for; matrix products, arithmetic and copies ran while one was open for 4% of the time, Pallas kernels for 0%

commit v1 on v0

v1 whole, which is shorter than its diff:
```python
import math

import jax
import jax.numpy as jnp
from jax import lax
from jax.experimental import pallas as pl
from jax.experimental.pallas import tpu as pltpu
from jax.sharding import PartitionSpec as P
HD=128; GROUP=12; PAIR=2; BLOCKS=9; KEYS=BLOCKS*128
BIG=float(2**20)
SCALE=1.0/math.sqrt(HD); LOG2E=math.log2(math.e)

def nt(a,b):
    return lax.dot_general(a,b,(((1,),(1,)),((),())),preferred_element_type=jnp.float32)
def nn(a,b):
    return jnp.dot(a,b,preferred_element_type=jnp.float32)

def kernel(head_ref, q_ref, own_ref, recv_ref, kmask_ref, qmask_ref, *rest):
    kv_refs=rest[:BLOCKS]
    keep_ref, send_ref, dq_ref = rest[BLOCKS:BLOCKS+3]
    g_refs=rest[BLOCKS+3:2*BLOCKS+3]
    kx, vv, kt, vt, dk, dv, qx, do = rest[2*BLOCKS+3:]
    c=pl.program_id(1)
    side=head_ref[0]
    R=PAIR*128
    @pl.when(c==0)
    def _():
        for d in range(BLOCKS):
            rows=pl.ds(d*128,128)
            kblk=kv_refs[d][:,0:128]; vblk=kv_refs[d][:,128:256]
            kx[rows,0:128]=kblk; kx[rows,128:256]=kmask_ref[rows,:]
            vv[rows,:]=vblk
            kt[:,rows]=kblk.T; vt[:,rows]=vblk.T
        dk[...]=jnp.zeros_like(dk); dv[...]=jnp.zeros_like(dv)
    mine=pl.multiple_of(side*64,64); other=pl.multiple_of(64-side*64,64)
    for g in range(PAIR):
        cols=slice(g*128,g*128+128)
        qx[g*128:(g+1)*128,0:128]=q_ref[:,cols]
        qx[g*128:(g+1)*128,128:256]=qmask_ref[...]
        do[pl.ds(pl.multiple_of(g*128+mine,64),64),:]=own_ref[:,cols]
        do[pl.ds(pl.multiple_of(g*128+other,64),64),:]=recv_ref[:,cols]
    s=nt(kx[...],qx[...])
    key=lax.broadcasted_iota(jnp.int32,(128,R),0); row=lax.broadcasted_iota(jnp.int32,(128,R),1)&127
    s0=jnp.where(key<=row,s[:128],-BIG)
    s=jnp.concatenate([s0,s[128:]],0)
    m=jnp.max(s,axis=0,keepdims=True)
    p=jnp.exp2((s-m)*(SCALE*LOG2E))
    l=jnp.sum(p,axis=0,keepdims=True)
    w=p*(1.0/l)
    wl=w.astype(jnp.bfloat16)
    ot=nn(vt[...],wl).astype(jnp.bfloat16)
    dov=do[...]
    delta=jnp.sum(dov.T.astype(jnp.float32)*ot.astype(jnp.float32),axis=0,keepdims=True)
    dp=nt(vv[...],dov)
    ds=(w*(dp-delta)).astype(jnp.bfloat16)
    dv[...]+=nn(wl,dov)
    dk[...]+=nn(ds,qx[:,0:128])
    dqt=(nn(kt[...],ds)*SCALE)
    o=ot.T; dq=dqt.T.astype(jnp.bfloat16)
    do[...]=o
    for g in range(PAIR):
        cols=slice(g*128,g*128+128)
        dq_ref[:,cols]=dq[g*128:(g+1)*128]
        keep_ref[:,cols]=do[pl.ds(pl.multiple_of(g*128+mine,64),64),:]
        send_ref[:,cols]=do[pl.ds(pl.multiple_of(g*128+other,64),64),:]
    @pl.when(c==GROUP//PAIR-1)
    def _():
        for d in range(BLOCKS):
            rows=pl.ds(d*128,128)
            g_refs[d][:,0:128]=(dk[rows,:]*SCALE).astype(g_refs[d].dtype)
            g_refs[d][:,128:256]=dv[rows,:].astype(g_refs[d].dtype)

def attend(side, q, grad_out, recv, kmask, qmask, kvs):
    W=PAIR*128; steps=GROUP//PAIR
    tile=pl.BlockSpec((128,256),lambda h,c,s:(0,h))
    grid_spec=pltpu.PrefetchScalarGridSpec(
        num_scalar_prefetch=1, grid=(4,steps),
        in_specs=[pl.BlockSpec((128,W),lambda h,c,s:(0,h*steps+c)),
                  pl.BlockSpec((64,W),lambda h,c,s:(0,s[0]*4*steps+h*steps+c)),
                  pl.BlockSpec((64,W),lambda h,c,s:(0,h*steps+c)),
                  pl.BlockSpec((KEYS,128),lambda h,c,s:(0,0)),
                  pl.BlockSpec((128,128),lambda h,c,s:(0,0))]+[tile]*BLOCKS,
        out_specs=[pl.BlockSpec((64,W),lambda h,c,s:(0,h*steps+c))]*2+[pl.BlockSpec((128,W),lambda h,c,s:(0,h*steps+c))]+[tile]*BLOCKS,
        scratch_shapes=[pltpu.VMEM((KEYS,256),jnp.bfloat16),pltpu.VMEM((KEYS,128),jnp.bfloat16),
            pltpu.VMEM((128,KEYS),jnp.bfloat16),pltpu.VMEM((128,KEYS),jnp.bfloat16),
            pltpu.VMEM((KEYS,128),jnp.float32),pltpu.VMEM((KEYS,128),jnp.float32),
            pltpu.VMEM((W,256),jnp.bfloat16),pltpu.VMEM((W,128),jnp.bfloat16)])
    bf=jnp.bfloat16
    return pl.pallas_call(kernel,grid_spec=grid_spec,
        out_shape=[jax.ShapeDtypeStruct((64,6144),bf)]*2+[jax.ShapeDtypeStruct((128,6144),bf)]+
          [jax.ShapeDtypeStruct((128,1024),jnp.float32 if d==0 else bf) for d in range(BLOCKS)],
        compiler_params=pltpu.CompilerParams(dimension_semantics=("arbitrary","arbitrary"),vmem_limit_bytes=48*2**20),
        name="attend")(side,q,grad_out,recv,kmask,qmask,*kvs)


def shift(value, steps):
    count = lax.axis_size("dp")
    return lax.ppermute(value, "dp", [(i, (i + steps) % count) for i in range(count)])


def swap(value):
    return lax.ppermute(value, "head", [(0, 1), (1, 0)])


def masks(segments, index):
    rows = 128
    padded = jnp.concatenate([jnp.full((8 * rows,), 32, jnp.int32), segments])
    window = lax.dynamic_slice_in_dim(padded, index * rows, KEYS, 0)
    blocks = window.reshape(BLOCKS, rows)[::-1].reshape(KEYS)
    mine = lax.dynamic_slice_in_dim(segments, index * rows, rows, 0)
    codes = jnp.arange(128, dtype=jnp.int32)
    key_mask = (blocks[:, None] == codes[None, :]).astype(jnp.bfloat16)
    query_mask = jnp.where((mine[:, None] == codes[None, :]) | (codes[None, :] > 32), 0.0, -BIG).astype(jnp.bfloat16)
    return key_mask, query_mask


def body(queries, keys, values, grad_out, segments):
    index = lax.axis_index("dp")
    side = lax.axis_index("head")
    half = grad_out.shape[1] // 2
    own = jnp.concatenate([a[:, h * HD:(h + 1) * HD] for h in range(4) for a in (keys, values)], axis=1)
    k2 = shift(own, 2)
    k6 = shift(own, 6)
    k1 = shift(own, 1)
    k7 = shift(own, 7)
    k8 = shift(own, 8)
    recv = swap(lax.dynamic_slice_in_dim(grad_out, (1 - side) * half, half, 1))
    k3 = shift(k2, 1)
    k5 = shift(k6, -1)
    k4 = shift(k2, 2)
    key_mask, query_mask = masks(segments, index)
    keep, send, grad_queries, *g = attend(
        side.astype(jnp.int32).reshape(1), queries, grad_out, recv, key_mask, query_mask,
        [own, k1, k2, k3, k4, k5, k6, k7, k8])
    f32 = jnp.float32
    add = lambda *a: sum(x.astype(f32) for x in a).astype(jnp.bfloat16)
    r3 = shift(g[3], -1)
    r5 = shift(g[5], 1)
    r4 = shift(g[4], -2)
    r1 = shift(g[1], -1)
    r7 = shift(g[7], -7)
    r8 = shift(g[8], -8)
    r2 = shift(add(g[2], r3, r4), -2)
    r6 = shift(add(g[6], r5), -6)
    total = add(g[0], r1, r2, r6, r7, r8).reshape(128, 4, 2, HD)
    other = swap(send)
    attention_out = jnp.where(side == 0, jnp.concatenate([keep, other], 1), jnp.concatenate([other, keep], 1))
    return (attention_out, grad_queries, total[:, :, 0].reshape(128, 4 * HD), total[:, :, 1].reshape(128, 4 * HD))


def solution(mesh):
    placed = (P("dp", "head"), P("dp", "head"), P("dp", "head"), P(("dp", "head"), None), P())
    return jax.shard_map(
        body,
        mesh=mesh,
        in_specs=placed,
        out_specs=(P(("dp", "head"), None), P("dp", "head"), P("dp", "head"), P("dp", "head")),
        check_vma=False,
    )
```

time: 410 us -> 161 us (0.39)
  the two profiles are of different devices: /device:TPU:25 before, /device:TPU:33 now
where the time goes in v1:
time: 161 us; the launch traced here: 160 us
  waiting for transfers between devices  51.2 us (32%)
  Pallas kernels  50.6 us (31%)
  starting transfers between devices  41 us (25%)
  local copies, waits for them, and re-layouts  13.3 us (8%)
  other arithmetic  3.26 us (2%)
    ppermute x16, waiting for transfers between devices, shift(): lax.ppermute(value, 'dp', [(i, (i + steps) % count) for i in range(count)])  51.2 us
    pallas_call x1, Pallas kernels, attend(): pl.pallas_call(kernel, grid_spec=grid_spec, out_shape=[jax.ShapeDtypeStru...  50.6 us
    ppermute x16, starting transfers between devices, shift(): lax.ppermute(value, 'dp', [(i, (i + steps) % count) for i in range(count)])  35.6 us
    unnamed x21, local copies, waits for them, and re-layouts  10.6 us
    ppermute x2, starting transfers between devices, swap(): return lax.ppermute(value, 'head', [(0, 1), (1, 0)])  5.42 us
  transfers between devices with their start and end apart: 18, of which 7 were waited for; matrix products, arithmetic and copies ran while one was open for 3% of the time, Pallas kernels for 0%

profile of v1, /device:TPU:33, one launch (start us, length us, event | category | flops | bytes accessed | tf_op | source)
XLA Modules:
  0.0 160.1 jit_solution(5827960074358785233)
XLA Ops:
  6.8 3.1 %collective-permute-start.2 = (bf16[128,1024]{1,0:T(8,128)(2,1)S(1)}, bf16[128,1024]{1,0:T(8,128)(2,1)S(1)}, u32[]{:S(2)}, u32[]{:S(2)}) collective-permute-start(bf16[128,1024]{1,0:T(8,128)(2,1)S(1)} %slice_dynamic-update-slice_fusion.rest_0_), channel_id=1, source_target_pairs={{0,4},{2,6},{4,8},{6,10},{8,12},{10,14},{12,16},{14,18},{16,20},{1... | collective-permute-start | bytes 786440 | tf_op jit(solution)/shard_map/ppermute | solution.py:98
  9.9 2.2 %collective-permute-start.5 = (bf16[128,1024]{1,0:T(8,128)(2,1)S(1)}, bf16[128,1024]{1,0:T(8,128)(2,1)S(1)}, u32[]{:S(2)}, u32[]{:S(2)}) collective-permute-start(bf16[128,1024]{1,0:T(8,128)(2,1)S(1)} %slice_dynamic-update-slice_fusion.rest_0_), channel_id=1, source_target_pairs={{0,12},{2,14},{4,16},{6,18},{8,20},{10,22},{12,24},{14,26},{16,28}... | collective-permute-start | bytes 786440 | tf_op jit(solution)/shard_map/ppermute | solution.py:98
  12.8 1.8 %collective-permute-start.7 = (bf16[128,1024]{1,0:T(8,128)(2,1)S(1)}, bf16[128,1024]{1,0:T(8,128)(2,1)S(1)}, u32[]{:S(2)}, u32[]{:S(2)}) collective-permute-start(bf16[128,1024]{1,0:T(8,128)(2,1)S(1)} %slice_dynamic-update-slice_fusion.rest_0_), channel_id=1, source_target_pairs={{0,14},{2,16},{4,18},{6,20},{8,22},{10,24},{12,26},{14,28},{16,30}... | collective-permute-start | bytes 786440 | tf_op jit(solution)/shard_map/ppermute | solution.py:98
  14.5 1.2 constant_dynamic-slice_fusion
  15.7 1.6 %collective-permute-start = (bf16[64,6144]{1,0:T(8,128)(2,1)S(1)}, bf16[64,6144]{1,0:T(8,128)(2,1)}, u32[]{:S(2)}, u32[]{:S(2)}) collective-permute-start(bf16[64,6144]{1,0:T(8,128)(2,1)S(1)} %constant_dynamic-slice_fusion), channel_id=1, source_target_pairs={{0,1},{1,0},{2,3},{3,2},{4,5},{5,4},{6,7},{7,6},{8,9},{9,8},{10,11... | collective-permute-start | bytes 2359304 | tf_op jit(solution)/shard_map/ppermute | solution.py:102
  17.6 11.4 %collective-permute-done.2.rest_2_ = bf16[128,1024]{1,0:T(8,128)(2,1)S(1)} collective-permute-done((bf16[128,1024]{1,0:T(8,128)(2,1)S(1)}, bf16[128,1024]{1,0:T(8,128)(2,1)S(1)}, u32[]{:S(2)}, u32[]{:S(2)}) %collective-permute-start.2) | collective-permute-done | bytes 262176 | tf_op jit(solution)/shard_map/ppermute | solution.py:98
  29.1 2.6 %collective-permute-start.3 = (bf16[128,1024]{1,0:T(8,128)(2,1)S(1)}, bf16[128,1024]{1,0:T(8,128)(2,1)S(1)}, u32[]{:S(2)}, u32[]{:S(2)}) collective-permute-start(bf16[128,1024]{1,0:T(8,128)(2,1)S(1)} %collective-permute-done.2.rest_2_), channel_id=1, source_target_pairs={{0,2},{2,4},{4,6},{6,8},{8,10},{10,12},{12,14},{14,16},{16,18},{18... | collective-permute-start | bytes 786440 | tf_op jit(solution)/shard_map/ppermute | solution.py:98
  32.2 4.3 %collective-permute-done.7.rest_7_ = bf16[128,1024]{1,0:T(8,128)(2,1)S(1)} collective-permute-done((bf16[128,1024]{1,0:T(8,128)(2,1)S(1)}, bf16[128,1024]{1,0:T(8,128)(2,1)S(1)}, u32[]{:S(2)}, u32[]{:S(2)}) %collective-permute-start.7) | collective-permute-done | bytes 262176 | tf_op jit(solution)/shard_map/ppermute | solution.py:98
  36.5 6.8 %collective-permute-start.6 = (bf16[128,1024]{1,0:T(8,128)(2,1)S(1)}, bf16[128,1024]{1,0:T(8,128)(2,1)S(1)}, u32[]{:S(2)}, u32[]{:S(2)}) collective-permute-start(bf16[128,1024]{1,0:T(8,128)(2,1)S(1)} %collective-permute-done.5.rest_6_), channel_id=1, source_target_pairs={{0,254},{2,0},{4,2},{6,4},{8,6},{10,8},{12,10},{14,12},{16,14},{18... | collective-permute-start | bytes 786440 | tf_op jit(solution)/shard_map/ppermute | solution.py:98
  43.5 8.7 %collective-permute-done.4.rest_4_ = bf16[128,1024]{1,0:T(8,128)(2,1)S(1)} collective-permute-done((bf16[128,1024]{1,0:T(8,128)(2,1)S(1)}, bf16[128,1024]{1,0:T(8,128)(2,1)S(1)}, u32[]{:S(2)}, u32[]{:S(2)}) %collective-permute-start.4) | collective-permute-done | bytes 262176 | tf_op jit(solution)/shard_map/ppermute | solution.py:98
  53.6 0.9 copy-done.1
  54.6 0.9 copy-done.3
  55.5 50.6 %attend.1 = (bf16[64,6144]{1,0:T(8,128)(2,1)S(1)}, bf16[64,6144]{1,0:T(8,128)(2,1)}, bf16[128,6144]{1,0:T(8,128)(2,1)}, f32[128,1024]{1,0:T(8,128)S(1)}, bf16[12...) custom-call(s32[1]{0:T(128)} %bitcast.head_ref, ...), custom_call_target="tpu_custom_call" | custom-call | tf_op jit(solution)/shard_map/attend/pallas_call | solution.py:89
  106.1 6.5 %collective-permute-start.11 = (bf16[128,1024]{1,0:T(8,128)(2,1)S(1)}, bf16[128,1024]{1,0:T(8,128)(2,1)S(1)}, u32[]{:S(2)}, u32[]{:S(2)}) collective-permute-start(bf16[128,1024]{1,0:T(8,128)(2,1)S(1)} %get-tuple-element.22), channel_id=1, source_target_pairs={{0,254},{2,0},{4,2},{6,4},{8,6},{10,8},{12,10},{14,12},{16,14},{18... | collective-permute-start | bytes 786440 | tf_op jit(solution)/shard_map/ppermute | solution.py:98
  112.6 1.3 collective-permute-start.14
  114.1 1.3 collective-permute-start.16
  115.4 3.8 %collective-permute-done.11 = bf16[128,1024]{1,0:T(8,128)(2,1)S(1)} collective-permute-done((bf16[128,1024]{1,0:T(8,128)(2,1)S(1)}, bf16[128,1024]{1,0:T(8,128)(2,1)S(1)}, u32[]{:S(2)}, u32[]{:S(2)}) %collective-permute-start.11) | collective-permute-done | bytes 262176 | tf_op jit(solution)/shard_map/ppermute | solution.py:98
  119.3 8.2 %collective-permute-done.12 = bf16[128,1024]{1,0:T(8,128)(2,1)S(1)} collective-permute-done((bf16[128,1024]{1,0:T(8,128)(2,1)S(1)}, bf16[128,1024]{1,0:T(8,128)(2,1)S(1)}, u32[]{:S(2)}, u32[]{:S(2)}) %collective-permute-start.12) | collective-permute-done | bytes 262176 | tf_op jit(solution)/shard_map/ppermute | solution.py:98
  127.5 3.8 %collective-permute-start.9 = (bf16[64,6144]{1,0:T(8,128)(2,1)}, bf16[64,6144]{1,0:T(8,128)(2,1)S(1)}, u32[]{:S(2)}, u32[]{:S(2)}) collective-permute-start(bf16[64,6144]{1,0:T(8,128)(2,1)} %get-tuple-element.17), channel_id=1, source_target_pairs={{0,1},{1,0},{2,3},{3,2},{4,5},{5,4},{6,7},{7,6},{8,9},{9,8},{10,11... | collective-permute-start | bytes 2359304 | tf_op jit(solution)/shard_map/ppermute | solution.py:102
  131.5 8.7 %collective-permute-start.13 = (bf16[128,1024]{1,0:T(8,128)(2,1)S(1)}, bf16[128,1024]{1,0:T(8,128)(2,1)}, u32[]{:S(2)}, u32[]{:S(2)}) collective-permute-start(bf16[128,1024]{1,0:T(8,128)(2,1)S(1)} %add_convert_fusion.2), channel_id=1, source_target_pairs={{0,252},{2,254},{4,0},{6,2},{8,4},{10,6},{12,8},{14,10},{16,12},{1... | collective-permute-start | bytes 786440 | tf_op jit(solution)/shard_map/ppermute | solution.py:98
  140.3 8.2 %collective-permute-done.13 = bf16[128,1024]{1,0:T(8,128)(2,1)} collective-permute-done((bf16[128,1024]{1,0:T(8,128)(2,1)S(1)}, bf16[128,1024]{1,0:T(8,128)(2,1)}, u32[]{:S(2)}, u32[]{:S(2)}) %collective-permute-start.13) | collective-permute-done | bytes 262176 | tf_op jit(solution)/shard_map/ppermute | solution.py:98
  148.5 6.4 %collective-permute-done.15 = bf16[128,1024]{1,0:T(8,128)(2,1)S(1)} collective-permute-done((bf16[128,1024]{1,0:T(8,128)(2,1)S(1)}, bf16[128,1024]{1,0:T(8,128)(2,1)S(1)}, u32[]{:S(2)}, u32[]{:S(2)}) %collective-permute-start.15) | collective-permute-done | bytes 262176 | tf_op jit(solution)/shard_map/ppermute | solution.py:98
  155.0 1.3 add_convert_fusion
  158.6 1.5 maximum_select_fusion
  (48 shorter events, 12.1 us)
Async XLA Ops:
  0.6 16.7 %copy-start.4 = (s32[16384]{0:T(1024)S(1)}, s32[16384]{0:T(1024)}, u32[]{:S(2)}) copy-start(s32[16384]{0:T(1024)} %param.9) | copy-start | bytes 196612
  6.8 22.2 %collective-permute-start.2 = (bf16[128,1024]{1,0:T(8,128)(2,1)S(1)}, bf16[128,1024]{1,0:T(8,128)(2,1)S(1)}, u32[]{:S(2)}, u32[]{:S(2)}) collective-permute-start(bf16[128,1024]{1,0:T(8,128)(2,1)S(1)} %slice_dynamic-update-slice_fusion.rest_0_), channel_id=1, source_target_pairs={{0,4},{2,6},{4,8},{6,10},{8,12},{10,14},{12,16},{14,18},{16,20},{1... | collective-permute-start | bytes 786440 | tf_op jit(solution)/shard_map/ppermute | solution.py:98
  9.9 19.2 %collective-permute-start.5 = (bf16[128,1024]{1,0:T(8,128)(2,1)S(1)}, bf16[128,1024]{1,0:T(8,128)(2,1)S(1)}, u32[]{:S(2)}, u32[]{:S(2)}) collective-permute-start(bf16[128,1024]{1,0:T(8,128)(2,1)S(1)} %slice_dynamic-update-slice_fusion.rest_0_), channel_id=1, source_target_pairs={{0,12},{2,14},{4,16},{6,18},{8,20},{10,22},{12,24},{14,26},{16,28}... | collective-permute-start | bytes 786440 | tf_op jit(solution)/shard_map/ppermute | solution.py:98
  12.1 19.6 %collective-permute-start.1 = (bf16[128,1024]{1,0:T(8,128)(2,1)S(1)}, bf16[128,1024]{1,0:T(8,128)(2,1)S(1)}, u32[]{:S(2)}, u32[]{:S(2)}) collective-permute-start(bf16[128,1024]{1,0:T(8,128)(2,1)S(1)} %slice_dynamic-update-slice_fusion.rest_0_), channel_id=1, source_target_pairs={{0,2},{2,4},{4,6},{6,8},{8,10},{10,12},{12,14},{14,16},{16,18},{18... | collective-permute-start | bytes 786440 | tf_op jit(solution)/shard_map/ppermute | solution.py:98
  12.8 23.7 %collective-permute-start.7 = (bf16[128,1024]{1,0:T(8,128)(2,1)S(1)}, bf16[128,1024]{1,0:T(8,128)(2,1)S(1)}, u32[]{:S(2)}, u32[]{:S(2)}) collective-permute-start(bf16[128,1024]{1,0:T(8,128)(2,1)S(1)} %slice_dynamic-update-slice_fusion.rest_0_), channel_id=1, source_target_pairs={{0,14},{2,16},{4,18},{6,20},{8,22},{10,24},{12,26},{14,28},{16,30}... | collective-permute-start | bytes 786440 | tf_op jit(solution)/shard_map/ppermute | solution.py:98
  15.7 37.9 %collective-permute-start = (bf16[64,6144]{1,0:T(8,128)(2,1)S(1)}, bf16[64,6144]{1,0:T(8,128)(2,1)}, u32[]{:S(2)}, u32[]{:S(2)}) collective-permute-start(bf16[64,6144]{1,0:T(8,128)(2,1)S(1)} %constant_dynamic-slice_fusion), channel_id=1, source_target_pairs={{0,1},{1,0},{2,3},{3,2},{4,5},{5,4},{6,7},{7,6},{8,9},{9,8},{10,11... | collective-permute-start | bytes 2359304 | tf_op jit(solution)/shard_map/ppermute | solution.py:102
  29.1 14.4 %collective-permute-start.8 = (bf16[128,1024]{1,0:T(8,128)(2,1)S(1)}, bf16[128,1024]{1,0:T(8,128)(2,1)S(1)}, u32[]{:S(2)}, u32[]{:S(2)}) collective-permute-start(bf16[128,1024]{1,0:T(8,128)(2,1)S(1)} %slice_dynamic-update-slice_fusion.rest_0_), channel_id=1, source_target_pairs={{0,16},{2,18},{4,20},{6,22},{8,24},{10,26},{12,28},{14,30},{16,32}... | collective-permute-start | bytes 786440 | tf_op jit(solution)/shard_map/ppermute | solution.py:98
  29.1 14.4 %collective-permute-start.3 = (bf16[128,1024]{1,0:T(8,128)(2,1)S(1)}, bf16[128,1024]{1,0:T(8,128)(2,1)S(1)}, u32[]{:S(2)}, u32[]{:S(2)}) collective-permute-start(bf16[128,1024]{1,0:T(8,128)(2,1)S(1)} %collective-permute-done.2.rest_2_), channel_id=1, source_target_pairs={{0,2},{2,4},{4,6},{6,8},{8,10},{10,12},{12,14},{14,16},{16,18},{18... | collective-permute-start | bytes 786440 | tf_op jit(solution)/shard_map/ppermute | solution.py:98
  31.7 20.5 %collective-permute-start.4 = (bf16[128,1024]{1,0:T(8,128)(2,1)S(1)}, bf16[128,1024]{1,0:T(8,128)(2,1)S(1)}, u32[]{:S(2)}, u32[]{:S(2)}) collective-permute-start(bf16[128,1024]{1,0:T(8,128)(2,1)S(1)} %collective-permute-done.2.rest_2_), channel_id=1, source_target_pairs={{0,4},{2,6},{4,8},{6,10},{8,12},{10,14},{12,16},{14,18},{16,20},{1... | collective-permute-start | bytes 786440 | tf_op jit(solution)/shard_map/ppermute | solution.py:98
  36.5 16.4 %collective-permute-start.6 = (bf16[128,1024]{1,0:T(8,128)(2,1)S(1)}, bf16[128,1024]{1,0:T(8,128)(2,1)S(1)}, u32[]{:S(2)}, u32[]{:S(2)}) collective-permute-start(bf16[128,1024]{1,0:T(8,128)(2,1)S(1)} %collective-permute-done.5.rest_6_), channel_id=1, source_target_pairs={{0,254},{2,0},{4,2},{6,4},{8,6},{10,8},{12,10},{14,12},{16,14},{18... | collective-permute-start | bytes 786440 | tf_op jit(solution)/shard_map/ppermute | solution.py:98
  52.2 0.7 copy-start
  52.9 0.7 copy-start.2
  53.6 1.0 copy-start.1
  54.5 0.9 copy-start.3
  106.1 13.1 %collective-permute-start.11 = (bf16[128,1024]{1,0:T(8,128)(2,1)S(1)}, bf16[128,1024]{1,0:T(8,128)(2,1)S(1)}, u32[]{:S(2)}, u32[]{:S(2)}) collective-permute-start(bf16[128,1024]{1,0:T(8,128)(2,1)S(1)} %get-tuple-element.22), channel_id=1, source_target_pairs={{0,254},{2,0},{4,2},{6,4},{8,6},{10,8},{12,10},{14,12},{16,14},{18... | collective-permute-start | bytes 786440 | tf_op jit(solution)/shard_map/ppermute | solution.py:98
  112.6 14.9 %collective-permute-start.12 = (bf16[128,1024]{1,0:T(8,128)(2,1)S(1)}, bf16[128,1024]{1,0:T(8,128)(2,1)S(1)}, u32[]{:S(2)}, u32[]{:S(2)}) collective-permute-start(bf16[128,1024]{1,0:T(8,128)(2,1)S(1)} %get-tuple-element.23), channel_id=1, source_target_pairs={{0,252},{2,254},{4,0},{6,2},{8,4},{10,6},{12,8},{14,10},{16,12},{1... | collective-permute-start | bytes 786440 | tf_op jit(solution)/shard_map/ppermute | solution.py:98
  112.6 18.8 %collective-permute-start.14 = (bf16[128,1024]{1,0:T(8,128)(2,1)S(1)}, bf16[128,1024]{1,0:T(8,128)(2,1)S(1)}, u32[]{:S(2)}, u32[]{:S(2)}) collective-permute-start(bf16[128,1024]{1,0:T(8,128)(2,1)S(1)} %get-tuple-element.25), channel_id=1, source_target_pairs={{0,2},{2,4},{4,6},{6,8},{8,10},{10,12},{12,14},{14,16},{16,18},{18... | collective-permute-start | bytes 786440 | tf_op jit(solution)/shard_map/ppermute | solution.py:98
  113.9 26.3 %collective-permute-start.10 = (bf16[128,1024]{1,0:T(8,128)(2,1)S(1)}, bf16[128,1024]{1,0:T(8,128)(2,1)S(1)}, u32[]{:S(2)}, u32[]{:S(2)}) collective-permute-start(bf16[128,1024]{1,0:T(8,128)(2,1)S(1)} %get-tuple-element.20), channel_id=1, source_target_pairs={{0,254},{2,0},{4,2},{6,4},{8,6},{10,8},{12,10},{14,12},{16,14},{18... | collective-permute-start | bytes 786440 | tf_op jit(solution)/shard_map/ppermute | solution.py:98
  114.1 26.2 %collective-permute-start.16 = (bf16[128,1024]{1,0:T(8,128)(2,1)}, bf16[128,1024]{1,0:T(8,128)(2,1)S(1)}, u32[]{:S(2)}, u32[]{:S(2)}) collective-permute-start(bf16[128,1024]{1,0:T(8,128)(2,1)} %get-tuple-element.26), channel_id=1, source_target_pairs={{0,242},{2,244},{4,246},{6,248},{8,250},{10,252},{12,254},{14,0},{... | collective-permute-start | bytes 786440 | tf_op jit(solution)/shard_map/ppermute | solution.py:98
  119.3 21.0 %collective-permute-start.17 = (bf16[128,1024]{1,0:T(8,128)(2,1)}, bf16[128,1024]{1,0:T(8,128)(2,1)}, u32[]{:S(2)}, u32[]{:S(2)}) collective-permute-start(bf16[128,1024]{1,0:T(8,128)(2,1)} %get-tuple-element.27), channel_id=1, source_target_pairs={{0,240},{2,242},{4,244},{6,246},{8,248},{10,250},{12,252},{14,254}... | collective-permute-start | bytes 786440 | tf_op jit(solution)/shard_map/ppermute | solution.py:98
  127.5 31.1 %collective-permute-start.9 = (bf16[64,6144]{1,0:T(8,128)(2,1)}, bf16[64,6144]{1,0:T(8,128)(2,1)S(1)}, u32[]{:S(2)}, u32[]{:S(2)}) collective-permute-start(bf16[64,6144]{1,0:T(8,128)(2,1)} %get-tuple-element.17), channel_id=1, source_target_pairs={{0,1},{1,0},{2,3},{3,2},{4,5},{5,4},{6,7},{7,6},{8,9},{9,8},{10,11... | collective-permute-start | bytes 2359304 | tf_op jit(solution)/shard_map/ppermute | solution.py:102
  131.5 17.1 %collective-permute-start.13 = (bf16[128,1024]{1,0:T(8,128)(2,1)S(1)}, bf16[128,1024]{1,0:T(8,128)(2,1)}, u32[]{:S(2)}, u32[]{:S(2)}) collective-permute-start(bf16[128,1024]{1,0:T(8,128)(2,1)S(1)} %add_convert_fusion.2), channel_id=1, source_target_pairs={{0,252},{2,254},{4,0},{6,2},{8,4},{10,6},{12,8},{14,10},{16,12},{1... | collective-permute-start | bytes 786440 | tf_op jit(solution)/shard_map/ppermute | solution.py:98
  140.2 14.8 %collective-permute-start.15 = (bf16[128,1024]{1,0:T(8,128)(2,1)S(1)}, bf16[128,1024]{1,0:T(8,128)(2,1)S(1)}, u32[]{:S(2)}, u32[]{:S(2)}) collective-permute-start(bf16[128,1024]{1,0:T(8,128)(2,1)S(1)} %add_convert_fusion.1), channel_id=1, source_target_pairs={{0,244},{2,246},{4,248},{6,250},{8,252},{10,254},{12,0},{14,2},{16... | collective-permute-start | bytes 786440 | tf_op jit(solution)/shard_map/ppermute | solution.py:98
